TPU v7x, 32 devices: a whole 2x2x4 slice. The times are simulated.
32 devices in a mesh: groups: 2 (over x), dp: 16 (over z, y, core).
Axes of the slice: x: 2, y: 2, z: 4, core: 2. Of those that a mesh axis runs over, the one named last changes fastest.
Arguments:
- tokens: bfloat16 [4096, 8192], P(('groups', 'dp')), parts along dimension 0, may hold values from -6 to 6
- tenant: int32 [4096], P(('groups', 'dp')), parts along dimension 0, may hold values from 0 to 7
- plan: int32 [4096, 1], P(('groups', 'dp')), parts along dimension 0, may hold values from 0 to 15; in each aligned block of 128 rows (0 to 127, 128 to 255, ...) at most 16 rows name the same one
- frozen_key_weight: bfloat16 [8192, 512], P('dp'), may hold values from -0.0625 to 0.0625
- adapter_down_weight: bfloat16 [8192, 128], P('dp'), may hold values from -0.0625 to 0.0625
- adapter_up_weight: bfloat16 [128, 512], replicated, may hold values from -1.5 to 1.5
- cotangent: bfloat16 [8192, 512], P(('groups', 'dp')), parts along dimension 0, may hold values from -6 to 6
Outputs:
- placed_out: bfloat16 [8192, 512], P(('groups', 'dp')), parts along dimension 0
- token_gradient: bfloat16 [4096, 8192], P(('groups', 'dp')), parts along dimension 0
- down_grad: float32 [16384, 128], P(('groups', 'dp')), parts along dimension 0
- up_weight_gradient: float32 [256, 512], P('groups'), parts along dimension 0
There are 2 independent parts, one for each index of `groups`. A program takes and returns all parts, laid end to end along the dimension named above; an argument that names none is the same for every part. Nothing has to cross between parts.
Inputs may be any that keep to these rules, and one draw needn't show every extreme that they name: `plan`: among the rows of one device, no device is named by more than 16 rows, and in every draw some device is named by exactly 16 rows of some device.
All inputs are finite; a program needn't handle non-finite values.
Results may differ from a plain program's by a relative error of at most 0.0047.
Values may be sent and summed in bfloat16 or wider, within the bound.
A program may use at most 64 MiB of HBM per device.

v0:
```python
import jax
import jax.numpy as jnp
from jax import lax
from jax.sharding import PartitionSpec as P

ADAPTER_RANK = 16


adapter_scale = 2.0


def place_rows(plan, slot_count, per_peer):
    destination = plan[:, 0]
    position = jnp.arange(destination.shape[0], dtype=jnp.int32)
    earlier_rows = (destination[None, :] == destination[:, None]) & (
        position[None, :] < position[:, None]
    )
    target_slot = destination * per_peer + jnp.sum(earlier_rows.astype(jnp.int32), axis=1)
    return (jnp.arange(slot_count, dtype=jnp.int32)[:, None] == target_slot[None, :]).astype(
        jnp.int32
    )


def tenant_mask(owners, feature_width):
    columns = jnp.arange(feature_width, dtype=jnp.int32) // ADAPTER_RANK
    return (columns[None, :] == owners[:, None]).astype(jnp.float32)


def leading_product(left, right):
    return lax.dot_general(
        left, right, (((0,), (0,)), ((), ())), preferred_element_type=jnp.float32
    )


def trailing_product(left, right):
    return lax.dot_general(
        left, right, (((1,), (1,)), ((), ())), preferred_element_type=jnp.float32
    )


def ahead_pass_rows(device_rows, tenant_picker, complete_weight, complete_down, adapter_up_weight):
    latent_state = (
        jnp.dot(device_rows, complete_down, preferred_element_type=jnp.float32) * tenant_picker
    ).astype(jnp.bfloat16)
    key_output = jnp.dot(device_rows, complete_weight, preferred_element_type=jnp.float32)
    key_output = key_output + adapter_scale * jnp.dot(
        latent_state, adapter_up_weight, preferred_element_type=jnp.float32
    )
    return (key_output.astype(jnp.bfloat16), latent_state)


def reverse_pass_rows(
    row_gradient, tenant_picker, complete_weight, complete_down, adapter_up_weight
):
    mixing_factor = (
        adapter_scale * trailing_product(row_gradient, adapter_up_weight) * tenant_picker
    ).astype(jnp.bfloat16)
    gradient = trailing_product(row_gradient, complete_weight) + trailing_product(
        mixing_factor, complete_down
    )
    return (mixing_factor, gradient.astype(jnp.bfloat16))


def shards(
    tokens, tenant, plan, frozen_key_weight, adapter_down_weight, adapter_up_weight, cotangent
):
    devices = lax.axis_size("dp")
    slot_count = cotangent.shape[0]
    per_peer = slot_count // devices
    feature_width = adapter_down_weight.shape[1]
    complete_weight, complete_down = (
        lax.all_gather(frozen_key_weight, "dp", axis=0, tiled=True),
        lax.all_gather(adapter_down_weight, "dp", axis=0, tiled=True),
    )
    onehot = place_rows(plan, slot_count, per_peer)
    selector_rows = onehot.astype(jnp.bfloat16)
    tenant_picker = tenant_mask(tenant, feature_width)
    key_output, latent_state = ahead_pass_rows(
        tokens, tenant_picker, complete_weight, complete_down, adapter_up_weight
    )
    send_out = jnp.dot(selector_rows, key_output, preferred_element_type=jnp.float32).astype(
        jnp.bfloat16
    )
    placed_out = lax.all_to_all(send_out, "dp", split_axis=0, concat_axis=0, tiled=True)
    returned_cot = lax.all_to_all(cotangent, "dp", split_axis=0, concat_axis=0, tiled=True)
    row_gradient = leading_product(selector_rows, returned_cot).astype(jnp.bfloat16)
    mixing_factor, token_gradient = reverse_pass_rows(
        row_gradient, tenant_picker, complete_weight, complete_down, adapter_up_weight
    )
    norm_multiplier = 1.0 / jnp.sqrt(jnp.float32(tokens.shape[0] * devices))
    up_portion = adapter_scale * leading_product(latent_state, row_gradient)
    down_part = leading_product(tokens, mixing_factor)
    down_grad = lax.psum_scatter(down_part, "dp", scatter_dimension=0, tiled=True) * norm_multiplier
    up_weight_gradient = lax.psum(up_portion, "dp") * norm_multiplier
    return (placed_out, token_gradient, down_grad, up_weight_gradient)


def solution(mesh):
    return jax.shard_map(
        shards,
        mesh=mesh,
        in_specs=(
            P(("groups", "dp"), None),
            P(("groups", "dp")),
            P(("groups", "dp"), None),
            P("dp", None),
            P("dp", None),
            P(),
            P(("groups", "dp"), None),
        ),
        out_specs=(
            P(("groups", "dp"), None),
            P(("groups", "dp"), None),
            P(("groups", "dp"), None),
            P("groups", None),
        ),
        check_vma=False,
    )
```

profile of v0, /device:TPU:0, one launch (start us, length us, event | category | flops | bytes accessed | tf_op | source)
XLA Modules:
  0.0 325.7 jit_solution(16550961274408275277)
XLA Ops:
  7.2 0.0 copy-start
  7.2 0.0 all-gather.5.cloned.1.call-start
  7.2 0.7 all-gather.5.cloned.1.call-update
  7.9 7.4 %all-to-all-start.1 = ((bf16[16,16,512]{2,1,0:T(8,128)(2,1)}), bf16[16,16,512]{2,1,0:T(8,128)(2,1)S(1)}, u32[]{:S(2)}, u32[]{:S(2)}) async-start(bf16[16,16,512]{2,1,0:T(8,128)(2,1)} %bitcast.27), calls=%async_computation.1 | async-start | bytes 524288 | tf_op jit(solution)/shard_map/all_to_all | solution.py:85
  15.3 0.0 all-reduce.2.cloned.1.call-start
  15.4 0.9 convert_reduce_fusion
  16.3 0.7 multiply_add_fusion
  17.0 8.4 %all-to-all-done.1 = bf16[16,16,512]{2,1,0:T(8,128)(2,1)S(1)} async-done(((bf16[16,16,512]{2,1,0:T(8,128)(2,1)}), bf16[16,16,512]{2,1,0:T(8,128)(2,1)S(1)}, u32[]{:S(2)}, u32[]{:S(2)}) %all-to-all-start.1) | async-done | bytes 262176 | tf_op jit(solution)/shard_map/all_to_all | solution.py:85
  25.4 0.2 convolution_convert_fusion.1
  25.6 1.1 fusion.5
  26.7 27.7 %all-gather.5.cloned.1.call-done = bf16[8192,128]{1,0:T(8,128)(2,1)} async-done(((bf16[512,128]{1,0:T(8,128)(2,1)}), bf16[8192,128]{1,0:T(8,128)(2,1)}) %all-gather.5.cloned.1.call-update) | async-done | bytes 2097168 | tf_op jit(solution)/shard_map/all_gather | solution.py:73
  54.4 2.3 fusion.4
  56.7 0.9 convolution_multiply_fusion
  57.6 0.0 all-reduce.2.cloned.1.call-update
  57.6 0.0 reduce-scatter.2.cloned.1.call-start
  57.7 2.7 convolution_bitcast_fusion
  60.4 0.0 reduce-scatter.2.cloned.1.call-update
  60.4 0.0 all-gather.3.cloned.1.call-start
  60.5 0.5 all-gather.3.cloned.1.call-update
  61.0 84.9 %all-reduce.2.cloned.1.call-done = f32[128,512]{1,0:T(8,128)} async-done(((f32[128,512]{1,0:T(8,128)}), f32[128,512]{1,0:T(8,128)}) %all-reduce.2.cloned.1.call-update) | async-done | bytes 262160 | tf_op jit(solution)/shard_map/psum | solution.py:94
  145.9 1.7 broadcast_multiply_fusion
  147.6 75.5 %reduce-scatter.2.cloned.1.call-done = f32[512,128]{0,1:T(8,128)} async-done(((f32[8192,128]{0,1:T(8,128)}), f32[512,128]{0,1:T(8,128)}) %reduce-scatter.2.cloned.1.call-update) | async-done | bytes 262160 | tf_op jit(solution)/shard_map/reduce_scatter | solution.py:93
  223.0 1.0 broadcast_multiply_fusion.1
  224.0 0.8 copy.12
  224.9 74.3 %all-gather.3.cloned.1.call-done = bf16[8192,512]{1,0:T(8,128)(2,1)} async-done(((bf16[512,512]{1,0:T(8,128)(2,1)}), bf16[8192,512]{1,0:T(8,128)(2,1)}) %all-gather.3.cloned.1.call-update) | async-done | bytes 8388624 | tf_op jit(solution)/shard_map/all_gather | solution.py:72
  299.2 4.6 %fusion.11 = f32[128,512]{1,0:T(8,128)S(1)} fusion(bf16[128,8192]{1,0:T(8,128)(2,1)S(1)} %copy-done, bf16[8192,512]{1,0:T(8,128)(2,1)} %all-gather.3.cloned.1.call-done), kind=kOutput, calls=%fused_computation.30 | convolution fusion | flops 1073741824 | bytes 10747904 | tf_op jit(solution)/shard_map/dot_general | solution.py:45
  303.9 1.1 convolution_convert_fusion
  304.9 3.5 %all-to-all-start = ((bf16[16,16,512]{2,1,0:T(8,128)(2,1)}), bf16[16,16,512]{2,1,0:T(8,128)(2,1)S(1)}, u32[]{:S(2)}, u32[]{:S(2)}) async-start(bf16[16,16,512]{2,1,0:T(8,128)(2,1)} %bitcast.1), calls=%async_computation | async-start | bytes 524288 | tf_op jit(solution)/shard_map/all_to_all | solution.py:84
  308.5 6.3 %fusion.12 = f32[128,8192]{1,0:T(8,128)S(1)} fusion(bf16[128,512]{1,0:T(8,128)(2,1)S(1)} %convolution_convert_fusion.1, bf16[8192,512]{1,0:T(8,128)(2,1)} %all-gather.3.cloned.1.call-done), kind=kOutput, calls=%fused_computation.31 | convolution fusion | flops 1073741824 | bytes 12713984 | tf_op jit(solution)/shard_map/dot_general | solution.py:36
  314.8 2.0 fusion
  316.9 1.6 all-to-all-done
  318.5 0.7 copy.15
  (6 shorter events, 0.0 us)
Async XLA Ops:
  7.2 47.2 %copy-start = (bf16[128,8192]{1,0:T(8,128)(2,1)S(1)}, bf16[128,8192]{1,0:T(8,128)(2,1)}, u32[]{:S(2)}) copy-start(bf16[128,8192]{1,0:T(8,128)(2,1)} %param.7) | copy-start | bytes 6291460
  7.2 47.2 %all-gather.5.cloned.1.call-start = ((), (), s32[]{:S(2)}) async-start(), calls=%async_computation.4 | async-start | bytes 2228224 | tf_op jit(solution)/shard_map/all_gather | solution.py:73
  7.9 17.5 %all-to-all-start.1 = ((bf16[16,16,512]{2,1,0:T(8,128)(2,1)}), bf16[16,16,512]{2,1,0:T(8,128)(2,1)S(1)}, u32[]{:S(2)}, u32[]{:S(2)}) async-start(bf16[16,16,512]{2,1,0:T(8,128)(2,1)} %bitcast.27), calls=%async_computation.1 | async-start | bytes 524288 | tf_op jit(solution)/shard_map/all_to_all | solution.py:85
  15.3 130.6 %all-reduce.2.cloned.1.call-start = ((), (), s32[]{:S(2)}) async-start(), calls=%async_computation.6 | async-start | bytes 524288 | tf_op jit(solution)/shard_map/psum | solution.py:94
  57.6 165.4 %reduce-scatter.2.cloned.1.call-start = ((), (), s32[]{:S(2)}) async-start(), calls=%async_computation.5 | async-start | bytes 4456448 | tf_op jit(solution)/shard_map/reduce_scatter | solution.py:93
  60.4 238.8 %all-gather.3.cloned.1.call-start = ((), (), s32[]{:S(2)}) async-start(), calls=%async_computation.3 | async-start | bytes 8912896 | tf_op jit(solution)/shard_map/all_gather | solution.py:72
  224.8 79.0 %copy-start.2 = (bf16[128,512]{1,0:T(8,128)(2,1)S(1)}, bf16[128,512]{1,0:T(8,128)(2,1)}, u32[]{:S(2)}) copy-start(bf16[128,512]{1,0:T(8,128)(2,1)} %param.12) | copy-start | bytes 393220
  304.9 13.5 %all-to-all-start = ((bf16[16,16,512]{2,1,0:T(8,128)(2,1)}), bf16[16,16,512]{2,1,0:T(8,128)(2,1)S(1)}, u32[]{:S(2)}, u32[]{:S(2)}) async-start(bf16[16,16,512]{2,1,0:T(8,128)(2,1)} %bitcast.1), calls=%async_computation | async-start | bytes 524288 | tf_op jit(solution)/shard_map/all_to_all | solution.py:84
  308.5 6.4 %copy-start.1 = (bf16[8192,128]{1,0:T(8,128)(2,1)S(1)}, bf16[8192,128]{1,0:T(8,128)(2,1)}, u32[]{:S(2)}) copy-start(bf16[8192,128]{1,0:T(8,128)(2,1)} %all-gather.5.cloned.1.call-done) | copy-start | bytes 6291460
Sparse Core Ops, SparseCore 0:
  10.2 44.1 all-gather.4
  58.4 87.4 all-reduce.1
  149.7 73.2 reduce-scatter.1
  225.3 73.8 all-gather.2
where the time goes:
time: 326 us
  waiting for transfers between devices  274 us (84%)
  matrix products  21.3 us (7%)
  between operations  13.9 us (4%)
  starting transfers between devices  11.1 us (3%)
  other arithmetic  4.23 us (1%)
    psum x1, waiting for transfers between devices, shards(): up_weight_gradient = lax.psum(up_portion, 'dp') * norm_multiplier  84.9 us
    reduce_scatter x1, waiting for transfers between devices, shards(): lax.psum_scatter(down_part, 'dp', scatter_dimension=0, tiled=True)  75.5 us
    all_gather x1, waiting for transfers between devices, shards(): lax.all_gather(frozen_key_weight, 'dp', axis=0, tiled=True)  74.3 us
    all_gather x1, waiting for transfers between devices, shards(): lax.all_gather(adapter_down_weight, 'dp', axis=0, tiled=True)  27.7 us
    dot_general x3, matrix products, trailing_product(): lax.dot_general(left, right, (((1,), (1,)), ((), ())), preferred_element_...  9.46 us
    all_to_all x1, waiting for transfers between devices, shards(): lax.all_to_all(cotangent, 'dp', split_axis=0, concat_axis=0, tiled=True)  8.43 us
    all_to_all x1, starting transfers between devices, shards(): lax.all_to_all(cotangent, 'dp', split_axis=0, concat_axis=0, tiled=True)  7.4 us
  transfers between devices with their start and end apart: 6, of which 6 were waited for; matrix products, arithmetic and copies ran while one was open for 5% of the time, Pallas kernels for 0%

commit v1 on v0

v1 whole, which is shorter than its diff:
```python
import functools

import jax
import jax.numpy as jnp
from jax import lax
from jax.experimental import pallas as pl
from jax.experimental.pallas import tpu as pltpu
from jax.sharding import PartitionSpec as P

ADAPTER_RANK = 16
SUBS = 2


adapter_scale = 2.0


def remote(src, dst, send_sem, recv_sem, target):
    return pltpu.make_async_remote_copy(
        src_ref=src,
        dst_ref=dst,
        send_sem=send_sem,
        recv_sem=recv_sem,
        device_id={"dp": target},
        device_id_type=pl.DeviceIdType.MESH,
    )


def greet_all(me, devices):
    barrier = pltpu.get_barrier_semaphore()
    for offset in range(1, devices):
        pl.semaphore_signal(
            barrier,
            inc=1,
            device_id={"dp": lax.rem(me + offset, devices)},
            device_id_type=pl.DeviceIdType.MESH,
        )
    pl.semaphore_wait(barrier, devices - 1)


def ring_position(chip, around):
    z, y = chip // 2, chip % 2
    return z + y * (around - 1 - 2 * z)


def ring_chip(position, around):
    back = position // (around // 2)
    return 2 * position + back * (2 * around - 1 - 4 * position)


def gather_kernel(
    devices, block_ref, cot_ref, full_ref, rows_ref,
    own_sem, own_cot_sem, ring_send, ring_recv, side_send, side_recv,
    own_side_send, own_side_recv, cot_send, cot_recv,
):
    me = lax.axis_index("dp")
    around = devices // 2
    chip, core = me // 2, me % 2
    sibling = chip * 2 + 1 - core
    spot = ring_position(chip, around)
    depth = block_ref.shape[0]
    piece = depth // (2 * SUBS)
    slots = cot_ref.shape[0] // devices

    def chip_at(hops):
        return ring_chip(lax.rem(spot + hops + around, around), around)

    def piece_of(device, way, sub):
        return full_ref.at[pl.ds(device * depth + (way * SUBS + sub) * piece, piece)]

    own = pltpu.make_async_copy(block_ref, full_ref.at[pl.ds(me * depth, depth)], own_sem)
    own.start()
    own_cot = pltpu.make_async_copy(
        cot_ref.at[pl.ds(me * slots, slots)], rows_ref.at[pl.ds(me * slots, slots)], own_cot_sem
    )
    own_cot.start()
    greet_all(me, devices)
    pending = []

    ways = (1, -1)
    for sub in range(SUBS):
        for way in range(2):
            source = block_ref.at[pl.ds((way * SUBS + sub) * piece, piece)]
            copy = remote(
                source, piece_of(me, way, sub), ring_send.at[way, sub, 0],
                ring_recv.at[way, sub, 0], chip_at(ways[way]) * 2 + core,
            )
            copy.start()
            pending.append(copy)
    side = remote(
        block_ref, full_ref.at[pl.ds(me * depth, depth)], own_side_send, own_side_recv, sibling
    )
    side.start()
    cots = []
    for offset in range(1, devices):
        peer = lax.rem(me + offset, devices)
        copy = remote(
            cot_ref.at[pl.ds(peer * slots, slots)], rows_ref.at[pl.ds(me * slots, slots)],
            cot_send.at[offset], cot_recv.at[offset], peer,
        )
        copy.start()
        cots.append(copy)

    sides = []
    for step in range(around - 1):
        for sub in range(SUBS):
            for way in range(2):
                origin = chip_at(-ways[way] * (step + 1))
                here = piece_of(origin * 2 + core, way, sub)
                remote(
                    here, here, ring_send.at[way, sub, step], ring_recv.at[way, sub, step], sibling
                ).wait_recv()
                if step < around - 2:
                    copy = remote(
                        here, here, ring_send.at[way, sub, step + 1],
                        ring_recv.at[way, sub, step + 1], chip_at(ways[way]) * 2 + core,
                    )
                    copy.start()
                    pending.append(copy)
                copy = remote(
                    here, here, side_send.at[way, sub, step], side_recv.at[way, sub, step], sibling
                )
                copy.start()
                sides.append((copy, piece_of(origin * 2 + 1 - core, way, sub), way, sub, step))

    own.wait()
    own_cot.wait()
    for offset in range(1, devices):
        cots[offset - 1].wait_send()
        origin = lax.rem(me - offset + devices, devices)
        place = rows_ref.at[pl.ds(origin * slots, slots)]
        remote(place, place, cot_send.at[offset], cot_recv.at[offset], sibling).wait_recv()
    for copy in pending:
        copy.wait_send()
    side.wait_send()
    place = full_ref.at[pl.ds(sibling * depth, depth)]
    remote(place, place, own_side_send, own_side_recv, sibling).wait_recv()
    for copy, place, way, sub, step in sides:
        copy.wait_send()
        remote(
            place, place, side_send.at[way, sub, step], side_recv.at[way, sub, step], sibling
        ).wait_recv()


def gather_blocks(devices, block, cotangent):
    dma = pltpu.SemaphoreType.DMA
    steps = devices // 2 - 1
    anywhere = pl.BlockSpec(memory_space=pl.ANY)
    return pl.pallas_call(
        functools.partial(gather_kernel, devices),
        out_shape=(
            jax.ShapeDtypeStruct((devices * block.shape[0], block.shape[1]), block.dtype),
            jax.ShapeDtypeStruct(cotangent.shape, cotangent.dtype),
        ),
        in_specs=[anywhere] * 2,
        out_specs=(anywhere, anywhere),
        scratch_shapes=[
            dma, dma,
            dma((2, SUBS, steps)), dma((2, SUBS, steps)),
            dma((2, SUBS, steps)), dma((2, SUBS, steps)),
            dma, dma,
            dma((devices,)), dma((devices,)),
        ],
        compiler_params=pltpu.CompilerParams(
            collective_id=0, has_side_effects=True, vmem_limit_bytes=48 * 1024 * 1024
        ),
    )(block, cotangent)


def finish_kernel(
    devices, scale, down_ref, up_ref, send_ref, down_out, up_out, placed_ref,
    side_buf, chip_buf, land_buf, up_buf, up_sum,
    own_sem, place_send, place_recv, up_send, up_recv, share_send, share_recv,
    side_send, side_recv, chip_send, chip_recv,
):
    me = lax.axis_index("dp")
    chips = devices // 2
    chip, core = me // 2, me % 2
    sibling = chip * 2 + 1 - core
    slots = send_ref.shape[0] // devices
    share = up_ref.shape[0] // devices

    own = pltpu.make_async_copy(
        send_ref.at[pl.ds(me * slots, slots)], placed_ref.at[pl.ds(me * slots, slots)], own_sem
    )
    own.start()
    greet_all(me, devices)

    sides = []
    for offset in list(range(1, chips)) + [0]:
        target = lax.rem(chip + offset, chips)
        copy = remote(
            down_ref.at[target * 2 + 1 - core], side_buf.at[offset],
            side_send.at[offset], side_recv.at[offset], sibling,
        )
        copy.start()
        sides.append(copy)
    ups, places = [], []
    for offset in range(1, devices):
        peer = lax.rem(me + offset, devices)
        copy = remote(
            up_ref.at[pl.ds(peer * share, share)], up_buf.at[offset],
            up_send.at[offset], up_recv.at[offset], peer,
        )
        copy.start()
        ups.append(copy)
    for offset in range(1, devices):
        peer = lax.rem(me + offset, devices)
        copy = remote(
            send_ref.at[pl.ds(peer * slots, slots)], placed_ref.at[pl.ds(me * slots, slots)],
            place_send.at[offset], place_recv.at[offset], peer,
        )
        copy.start()
        places.append(copy)

    sent = []
    for offset in range(1, chips):
        target = lax.rem(chip + offset, chips)
        sides[offset - 1].wait()
        chip_buf[offset] = (down_ref[target * 2 + core] + side_buf[offset]).astype(jnp.bfloat16)
        copy = remote(
            chip_buf.at[offset], land_buf.at[offset],
            chip_send.at[offset], chip_recv.at[offset], target * 2 + core,
        )
        copy.start()
        sent.append(copy)

    total = up_ref[pl.ds(pl.multiple_of(me * share, share), share), :]
    for offset in range(1, devices):
        ups[offset - 1].wait()
        total = total + up_buf[offset]
    up_sum[...] = total * scale
    up_out[pl.ds(pl.multiple_of(me * share, share), share), :] = total * scale
    shares = []
    for offset in range(1, devices):
        peer = lax.rem(me + offset, devices)
        copy = remote(
            up_sum, up_out.at[pl.ds(me * share, share)],
            share_send.at[offset], share_recv.at[offset], peer,
        )
        copy.start()
        shares.append(copy)

    sides[chips - 1].wait()
    down_out[...] = down_ref[me] + side_buf[0]
    for offset in range(1, chips):
        sent[offset - 1].wait()
        down_out[...] += land_buf[offset].astype(jnp.float32)
    down_out[...] *= scale

    own.wait()
    for offset in range(1, devices):
        origin = lax.rem(me - offset + devices, devices)
        places[offset - 1].wait_send()
        place = placed_ref.at[pl.ds(origin * slots, slots)]
        remote(place, place, place_send.at[offset], place_recv.at[offset], sibling).wait_recv()
        shares[offset - 1].wait_send()
        place = up_out.at[pl.ds(origin * share, share)]
        remote(place, place, share_send.at[offset], share_recv.at[offset], sibling).wait_recv()


def finish(devices, scale, down_part, up_portion, send_out):
    dma = pltpu.SemaphoreType.DMA
    chips = devices // 2
    depth, width = down_part.shape[0] // devices, down_part.shape[1]
    share, features = up_portion.shape[0] // devices, up_portion.shape[1]
    anywhere = pl.BlockSpec(memory_space=pl.ANY)
    local = pl.BlockSpec(memory_space=pltpu.VMEM)
    return pl.pallas_call(
        functools.partial(finish_kernel, devices, scale),
        out_shape=(
            jax.ShapeDtypeStruct((depth, width), jnp.float32),
            jax.ShapeDtypeStruct(up_portion.shape, jnp.float32),
            jax.ShapeDtypeStruct(send_out.shape, send_out.dtype),
        ),
        in_specs=[local, local, anywhere],
        out_specs=(local, local, anywhere),
        scratch_shapes=[
            pltpu.VMEM((chips, depth, width), jnp.float32),
            pltpu.VMEM((chips, depth, width), jnp.bfloat16),
            pltpu.VMEM((chips, depth, width), jnp.bfloat16),
            pltpu.VMEM((devices, share, features), jnp.float32),
            pltpu.VMEM((share, features), jnp.float32),
            dma,
            dma((devices,)), dma((devices,)),
            dma((devices,)), dma((devices,)),
            dma((devices,)), dma((devices,)),
            dma((chips,)), dma((chips,)),
            dma((chips,)), dma((chips,)),
        ],
        compiler_params=pltpu.CompilerParams(
            collective_id=1, has_side_effects=True, vmem_limit_bytes=48 * 1024 * 1024
        ),
    )(down_part.reshape(devices, depth, width), up_portion, send_out)


def place_rows(plan, slot_count, per_peer):
    destination = plan[:, 0]
    position = jnp.arange(destination.shape[0], dtype=jnp.int32)
    earlier_rows = (destination[None, :] == destination[:, None]) & (
        position[None, :] < position[:, None]
    )
    target_slot = destination * per_peer + jnp.sum(earlier_rows.astype(jnp.int32), axis=1)
    return (jnp.arange(slot_count, dtype=jnp.int32)[:, None] == target_slot[None, :]).astype(
        jnp.int32
    )


def tenant_mask(owners, feature_width):
    columns = jnp.arange(feature_width, dtype=jnp.int32) // ADAPTER_RANK
    return (columns[None, :] == owners[:, None]).astype(jnp.float32)


def leading_product(left, right):
    return lax.dot_general(
        left, right, (((0,), (0,)), ((), ())), preferred_element_type=jnp.float32
    )


def trailing_product(left, right):
    return lax.dot_general(
        left, right, (((1,), (1,)), ((), ())), preferred_element_type=jnp.float32
    )


def shards(
    tokens, tenant, plan, frozen_key_weight, adapter_down_weight, adapter_up_weight, cotangent
):
    devices = lax.axis_size("dp")
    slot_count = cotangent.shape[0]
    per_peer = slot_count // devices
    features = frozen_key_weight.shape[1]
    feature_width = adapter_down_weight.shape[1]
    direct = devices == 16
    block = jnp.concatenate([frozen_key_weight, adapter_down_weight], axis=1)
    if direct:
        complete, returned_cot = gather_blocks(devices, block, cotangent)
    else:
        complete = lax.all_gather(block, "dp", axis=0, tiled=True)
        returned_cot = lax.all_to_all(cotangent, "dp", split_axis=0, concat_axis=0, tiled=True)
    selector_rows = place_rows(plan, slot_count, per_peer).astype(jnp.bfloat16)
    tenant_picker = tenant_mask(tenant, feature_width)
    both = jnp.dot(tokens, complete, preferred_element_type=jnp.float32)
    latent_state = (both[:, features:] * tenant_picker).astype(jnp.bfloat16)
    key_output = (
        both[:, :features]
        + adapter_scale
        * jnp.dot(latent_state, adapter_up_weight, preferred_element_type=jnp.float32)
    ).astype(jnp.bfloat16)
    send_out = jnp.dot(selector_rows, key_output, preferred_element_type=jnp.float32).astype(
        jnp.bfloat16
    )
    row_gradient = leading_product(selector_rows, returned_cot).astype(jnp.bfloat16)
    mixing_factor = (
        adapter_scale * trailing_product(row_gradient, adapter_up_weight) * tenant_picker
    ).astype(jnp.bfloat16)
    token_gradient = trailing_product(
        jnp.concatenate([row_gradient, mixing_factor], axis=1), complete
    ).astype(jnp.bfloat16)
    scale = (tokens.shape[0] * devices) ** -0.5
    up_portion = adapter_scale * leading_product(latent_state, row_gradient)
    down_part = leading_product(tokens, mixing_factor)
    if direct:
        down_grad, up_weight_gradient, placed_out = finish(
            devices, scale, down_part, up_portion, send_out
        )
    else:
        placed_out = lax.all_to_all(send_out, "dp", split_axis=0, concat_axis=0, tiled=True)
        down_grad = lax.psum_scatter(down_part, "dp", scatter_dimension=0, tiled=True) * scale
        up_weight_gradient = lax.psum(up_portion, "dp") * scale
    return (placed_out, token_gradient, down_grad, up_weight_gradient)


def solution(mesh):
    return jax.shard_map(
        shards,
        mesh=mesh,
        in_specs=(
            P(("groups", "dp"), None),
            P(("groups", "dp")),
            P(("groups", "dp"), None),
            P("dp", None),
            P("dp", None),
            P(),
            P(("groups", "dp"), None),
        ),
        out_specs=(
            P(("groups", "dp"), None),
            P(("groups", "dp"), None),
            P(("groups", "dp"), None),
            P("groups", None),
        ),
        check_vma=False,
    )
```

time: 326 us -> 138 us (0.42)
  waiting for transfers between devices: 274 us -> 0 us
  Pallas kernels: 0 us -> 108 us
  between operations: 13.9 us -> 0.78 us
  starting transfers between devices: 11.1 us -> 0 us
  local copies, waits for them, and re-layouts: 1.56 us -> 11.8 us
  matrix products: 21.3 us -> 14.5 us
    pallas_call x0 -> x2, Pallas kernels: none -> 108 us  [the longest x1 63.7 us: gather_blocks(): pl.pallas_call(functools.partial(gather_kernel, devices), out_shape=(jax....]
    all_gather x2 -> x0, waiting for transfers between devices: 102 us -> none  [the longest x1 74.3 us: shards(): lax.all_gather(frozen_key_weight, 'dp', axis=0, tiled=True)]
    psum x1 -> x0, waiting for transfers between devices: 84.9 us -> none  [shards(): up_weight_gradient = lax.psum(up_portion, 'dp') * norm_multiplier]
    reduce_scatter x1 -> x0, waiting for transfers between devices: 75.5 us -> none  [shards(): lax.psum_scatter(down_part, 'dp', scatter_dimension=0, tiled=True)]
    all_to_all x2 -> x0, starting transfers between devices: 10.9 us -> none  [the longest x1 7.4 us: shards(): lax.all_to_all(cotangent, 'dp', split_axis=0, concat_axis=0, tiled=True)]
    all_to_all x2 -> x0, waiting for transfers between devices: 10.1 us -> none  [the longest x1 8.43 us: shards(): lax.all_to_all(cotangent, 'dp', split_axis=0, concat_axis=0, tiled=True)]
    dot_general x0 -> x1, local copies, waits for them, and re-layouts: none -> 5.6 us  [leading_product(): lax.dot_general(left, right, (((0,), (0,)), ((), ())), preferred_element_...]
    unnamed x8 -> x19, local copies, waits for them, and re-layouts: 1.56 us -> 6.19 us
  transfers between devices with their start and end apart: 6 -> 0, of which waited for: 6 -> 0; matrix products, arithmetic and copies ran while one was open for 5% -> 0% of each run, Pallas kernels for 0% -> 0%
where the time goes in v1:
time: 138 us
  Pallas kernels  108 us (78%)
  matrix products  14.5 us (11%)
  local copies, waits for them, and re-layouts  11.8 us (9%)
  other arithmetic  2.83 us (2%)
    pallas_call x1, Pallas kernels, gather_blocks(): pl.pallas_call(functools.partial(gather_kernel, devices), out_shape=(jax....  63.7 us
    pallas_call x1, Pallas kernels, finish(): pl.pallas_call(functools.partial(finish_kernel, devices, scale), out_shap...  44.1 us
    unnamed x19, local copies, waits for them, and re-layouts  6.19 us
    dot_general x1, matrix products, shards(): both = jnp.dot(tokens, complete, preferred_element_type=jnp.float32)  5.93 us
    dot_general x1, local copies, waits for them, and re-layouts, leading_product(): lax.dot_general(left, right, (((0,), (0,)), ((), ())), preferred_element_...  5.6 us
    dot_general x2, matrix products, trailing_product(): lax.dot_general(left, right, (((1,), (1,)), ((), ())), preferred_element_...  4.93 us
    dot_general x3, matrix products, leading_product(): lax.dot_general(left, right, (((0,), (0,)), ((), ())), preferred_element_...  3.17 us

profile of v1, /device:TPU:0, one launch (start us, length us, event | category | flops | bytes accessed | tf_op | source)
XLA Modules:
  0.0 137.7 jit_solution(6759144585956017452)
XLA Ops:
  0.6 0.0 copy-start
  0.6 0.0 copy-start.4
  0.7 0.0 copy-start.3
  0.7 1.0 convert_reduce_fusion
  1.7 0.7 and_select_fusion
  2.3 1.2 pad_maximum_fusion.block_ref
  3.5 0.0 copy-start.2
  3.5 0.9 copy-done.2
  4.5 63.7 %shard_map.102 = (bf16[8192,640]{1,0:T(8,128)(2,1)}, bf16[256,512]{1,0:T(8,128)(2,1)S(1)}) custom-call(bf16[512,640]{1,0:T(8,128)(2,1)S(1)} %pad_maximum_fusion.block_ref, bf16[256,512]{1,0:T(8,128)(2,1)S(1)} %copy-done.2), custom_call_target="tpu_custom_call" | custom-call | tf_op jit(solution)/shard_map/pallas_call | solution.py:148
  68.2 0.2 convolution_convert_fusion.2
  68.4 0.0 copy-done.4
  68.4 0.0 copy-done.3
  68.5 0.0 slice-start
  68.5 0.2 fusion.3
  68.7 0.0 copy-done
  68.7 0.0 slice-start.1
  68.7 0.0 slice-start.2
  68.7 5.9 %convolution_bitcast_fusion.1 = f32[128,640]{1,0:T(8,128)S(1)} fusion(bf16[128,8192]{1,0:T(8,128)(2,1)S(1)} %copy-done, bf16[8192,640]{1,0:T(8,128)(2,1)} %get-tuple-element.10), kind=kOutput, calls=%fused_computation.3 | convolution fusion | flops 1342177280 | bytes 12910592 | tf_op jit(solution)/shard_map/dot_general | solution.py:342
  74.6 0.0 slice-done
  74.6 0.3 slice-done.1
  75.0 0.6 slice-done.2
  75.6 4.7 %convolution_convert_fusion = bf16[128,8192]{1,0:T(8,128)(2,1)} fusion(bf16[8192,640]{1,0:T(8,128)(2,1)S(1)} %bitcast.19, bf16[128,128]{1,0:T(8,128)(2,1)S(1)} %fusion.3, bf16[128,512]{1,0:T(8,128)(2,1)S(1)} %convolution_convert_fusion.2), kind=kOutput, calls=%fused_computation.1 | convolution fusion | flops 1343553536 | bytes 12746752 | tf_op jit(solution)/shard_map/dot_general | solution.py:320
  80.3 0.3 convolution_multiply_fusion.1.up_ref
  80.6 0.4 convolution_convert_fusion.1.send_ref
  81.0 2.7 %convolution_bitcast_fusion = f32[8192,128]{0,1:T(8,128)} fusion(bf16[128,128]{1,0:T(8,128)(2,1)S(1)} %fusion.3, bf16[128,8192]{1,0:T(8,128)(2,1)S(1)} %copy-done), kind=kOutput, calls=%fused_computation | convolution fusion | flops 268435456 | bytes 6324224 | tf_op jit(solution)/shard_map/dot_general | solution.py:314
  83.7 5.6 %copy.15 = f32[8192,128]{1,0:T(8,128)} copy(f32[8192,128]{0,1:T(8,128)} %convolution_bitcast_fusion) | data formatting | bytes 8388608 | tf_op jit(solution)/shard_map/dot_general | solution.py:314
  89.3 0.0 copy-start.1
  89.3 2.2 %copy-done.1 = f32[8192,128]{1,0:T(8,128)S(1)} copy-done((f32[8192,128]{1,0:T(8,128)S(1)}, f32[8192,128]{1,0:T(8,128)}, u32[]{:S(2)}) %copy-start.1) | copy-done | bytes 4194328
  91.5 44.1 %shard_map.103 = (f32[512,128]{1,0:T(8,128)S(1)}, f32[128,512]{1,0:T(8,128)S(1)}, bf16[256,512]{1,0:T(8,128)(2,1)S(1)}) custom-call(f32[16,512,128]{2,1,0:T(8,128)S(1)} %bitcast.17, f32[128,512]{1,0:T(8,128)S(1)} %convolution_multiply_fusion.1.up_ref, bf16[256,512]{1,0:T(8,128)(2,1)S(1)} %convolution_convert_fusion.1.send_ref), custom_call_target="tpu_custom_call" | custom-call | tf_op jit(solution)/shard_map/pallas_call | solution.py:268
  135.6 0.7 copy.22
  136.3 0.7 copy.23
  137.0 0.7 copy.24
  (1 shorter events, 0.0 us)
Async XLA Ops:
  0.6 68.0 %copy-start = (bf16[128,8192]{1,0:T(8,128)(2,1)S(1)}, bf16[128,8192]{1,0:T(8,128)(2,1)}, u32[]{:S(2)}) copy-start(bf16[128,8192]{1,0:T(8,128)(2,1)} %param.7) | copy-start | bytes 6291460
  0.6 67.8 %copy-start.4 = (s32[128]{0:T(128)S(1)}, s32[128]{0:T(128)}, u32[]{:S(2)}) copy-start(s32[128]{0:T(128)} %param.8) | copy-start | bytes 1540
  0.7 67.8 %copy-start.3 = (bf16[128,512]{1,0:T(8,128)(2,1)S(1)}, bf16[128,512]{1,0:T(8,128)(2,1)}, u32[]{:S(2)}) copy-start(bf16[128,512]{1,0:T(8,128)(2,1)} %param.12) | copy-start | bytes 393220
  3.5 1.0 copy-start.2
  68.5 6.2 %slice-start = ((s8[10485760]{0:T(1024)(128)(4,1)}), s8[4194304]{0:T(1024)(128)(4,1)S(1)}, s32[]{:S(2)}) async-start(s8[10485760]{0:T(1024)(128)(4,1)} %bitcast.18), calls=%async_computation | async-start | bytes 8388608
  68.7 6.3 %slice-start.1 = ((s8[10485760]{0:T(1024)(128)(4,1)}), s8[4194304]{0:T(1024)(128)(4,1)S(1)}, s32[]{:S(2)}) async-start(s8[10485760]{0:T(1024)(128)(4,1)} %bitcast.18), calls=%async_computation.1 | async-start | bytes 8388608
  68.7 6.9 %slice-start.2 = ((s8[10485760]{0:T(1024)(128)(4,1)}), s8[2097152]{0:T(1024)(128)(4,1)S(1)}, s32[]{:S(2)}) async-start(s8[10485760]{0:T(1024)(128)(4,1)} %bitcast.18), calls=%async_computation.2 | async-start | bytes 4194304
  89.3 2.2 %copy-start.1 = (f32[8192,128]{1,0:T(8,128)S(1)}, f32[8192,128]{1,0:T(8,128)}, u32[]{:S(2)}) copy-start(f32[8192,128]{1,0:T(8,128)} %copy.15) | copy-start | bytes 12582916

commit v2 on v1

--- a/solution.py
+++ b/solution.py
@@ -14,27 +14,27 @@
 adapter_scale = 2.0
 
 
-def remote(src, dst, send_sem, recv_sem, target):
+def remote(src, dst, send_sem, recv_sem, target, axis="dp"):
     return pltpu.make_async_remote_copy(
         src_ref=src,
         dst_ref=dst,
         send_sem=send_sem,
         recv_sem=recv_sem,
-        device_id={"dp": target},
+        device_id={axis: target},
         device_id_type=pl.DeviceIdType.MESH,
     )
 
 
-def greet_all(me, devices):
+def greet_all(me, devices, twin=None):
     barrier = pltpu.get_barrier_semaphore()
-    for offset in range(1, devices):
+    targets = [{"dp": lax.rem(me + offset, devices)} for offset in range(1, devices)]
+    if twin is not None:
+        targets.append({"groups": twin})
+    for target in targets:
         pl.semaphore_signal(
-            barrier,
-            inc=1,
-            device_id={"dp": lax.rem(me + offset, devices)},
-            device_id_type=pl.DeviceIdType.MESH,
-        )
-    pl.semaphore_wait(barrier, devices - 1)
+            barrier, inc=1, device_id=target, device_id_type=pl.DeviceIdType.MESH
+        )
+    pl.semaphore_wait(barrier, len(targets))
 
 
 def ring_position(chip, around):
@@ -51,6 +51,7 @@
     devices, block_ref, cot_ref, full_ref, rows_ref,
     own_sem, own_cot_sem, ring_send, ring_recv, side_send, side_recv,
     own_side_send, own_side_recv, cot_send, cot_recv,
+    twin_send, twin_recv, twin_side_send, twin_side_recv,
 ):
     me = lax.axis_index("dp")
     around = devices // 2
@@ -58,14 +59,22 @@
     sibling = chip * 2 + 1 - core
     spot = ring_position(chip, around)
     depth = block_ref.shape[0]
-    piece = depth // (2 * SUBS)
+    group = lax.axis_index("groups")
+    single = depth * 5 // 32
+    double = depth // 2 - 2 * single
     slots = cot_ref.shape[0] // devices
 
     def chip_at(hops):
         return ring_chip(lax.rem(spot + hops + around, around), around)
 
-    def piece_of(device, way, sub):
-        return full_ref.at[pl.ds(device * depth + (way * SUBS + sub) * piece, piece)]
+    def rows_of(way, sub, holder):
+        if sub == 0:
+            return holder * (depth - 2 * single) + way * single, single
+        return 2 * single + way * double, double
+
+    def piece_of(device, way, sub, holder):
+        first, count = rows_of(way, sub, holder)
+        return full_ref.at[pl.ds(device * depth + first, count)]
 
     own = pltpu.make_async_copy(block_ref, full_ref.at[pl.ds(me * depth, depth)], own_sem)
     own.start()
@@ -73,15 +82,15 @@
         cot_ref.at[pl.ds(me * slots, slots)], rows_ref.at[pl.ds(me * slots, slots)], own_cot_sem
     )
     own_cot.start()
-    greet_all(me, devices)
+    greet_all(me, devices, 1 - group)
     pending = []
 
     ways = (1, -1)
     for sub in range(SUBS):
         for way in range(2):
-            source = block_ref.at[pl.ds((way * SUBS + sub) * piece, piece)]
+            first, count = rows_of(way, sub, group)
             copy = remote(
-                source, piece_of(me, way, sub), ring_send.at[way, sub, 0],
+                block_ref.at[pl.ds(first, count)], piece_of(me, way, sub, group), ring_send.at[way, sub, 0],
                 ring_recv.at[way, sub, 0], chip_at(ways[way]) * 2 + core,
             )
             copy.start()
@@ -101,11 +110,24 @@
         cots.append(copy)
 
     sides = []
+
+    def relay_twin(step):
+        for way in range(2):
+            origin = chip_at(-ways[way] * (step + 1))
+            here = piece_of(origin * 2 + core, way, 0, 1 - group)
+            remote(
+                here, here, twin_send.at[way, step], twin_recv.at[way, step], 1 - group, "groups"
+            ).wait_recv()
+            sems = twin_side_send.at[way, step], twin_side_recv.at[way, step]
+            copy = remote(here, here, *sems, sibling)
+            copy.start()
+            sides.append((copy, piece_of(origin * 2 + 1 - core, way, 0, 1 - group), *sems))
+
     for step in range(around - 1):
         for sub in range(SUBS):
             for way in range(2):
                 origin = chip_at(-ways[way] * (step + 1))
-                here = piece_of(origin * 2 + core, way, sub)
+                here = piece_of(origin * 2 + core, way, sub, group)
                 remote(
                     here, here, ring_send.at[way, sub, step], ring_recv.at[way, sub, step], sibling
                 ).wait_recv()
@@ -116,11 +138,20 @@
                     )
                     copy.start()
                     pending.append(copy)
-                copy = remote(
-                    here, here, side_send.at[way, sub, step], side_recv.at[way, sub, step], sibling
-                )
+                if sub == 0:
+                    copy = remote(
+                        here, here, twin_send.at[way, step], twin_recv.at[way, step],
+                        1 - group, "groups",
+                    )
+                    copy.start()
+                    pending.append(copy)
+                sems = side_send.at[way, sub, step], side_recv.at[way, sub, step]
+                copy = remote(here, here, *sems, sibling)
                 copy.start()
-                sides.append((copy, piece_of(origin * 2 + 1 - core, way, sub), way, sub, step))
+                sides.append((copy, piece_of(origin * 2 + 1 - core, way, sub, group), *sems))
+        if step > 0:
+            relay_twin(step - 1)
+    relay_twin(around - 2)
 
     own.wait()
     own_cot.wait()
@@ -134,11 +165,9 @@
     side.wait_send()
     place = full_ref.at[pl.ds(sibling * depth, depth)]
     remote(place, place, own_side_send, own_side_recv, sibling).wait_recv()
-    for copy, place, way, sub, step in sides:
+    for copy, place, send_sem, recv_sem in sides:
         copy.wait_send()
-        remote(
-            place, place, side_send.at[way, sub, step], side_recv.at[way, sub, step], sibling
-        ).wait_recv()
+        remote(place, place, send_sem, recv_sem, sibling).wait_recv()
 
 
 def gather_blocks(devices, block, cotangent):
@@ -159,6 +188,8 @@
             dma((2, SUBS, steps)), dma((2, SUBS, steps)),
             dma, dma,
             dma((devices,)), dma((devices,)),
+            dma((2, steps)), dma((2, steps)),
+            dma((2, steps)), dma((2, steps)),
         ],
         compiler_params=pltpu.CompilerParams(
             collective_id=0, has_side_effects=True, vmem_limit_bytes=48 * 1024 * 1024
@@ -167,17 +198,27 @@
 
 
 def finish_kernel(
-    devices, scale, down_ref, up_ref, send_ref, down_out, up_out, placed_ref,
-    side_buf, chip_buf, land_buf, up_buf, up_sum,
-    own_sem, place_send, place_recv, up_send, up_recv, share_send, share_recv,
-    side_send, side_recv, chip_send, chip_recv,
+    devices, scale, tokens_ref, mix_ref, up_ref, send_ref, down_out, up_out, placed_ref,
+    part_buf, side_buf, y_buf, y_land, z_buf, z_land, up_side, up_buf, up_land,
+    own_sem, place_send, place_recv, side_send, side_recv, y_send, y_recv, z_send, z_recv,
+    up_side_send, up_side_recv, up_send, up_recv, share_send, share_recv, last_send, last_recv,
 ):
     me = lax.axis_index("dp")
-    chips = devices // 2
+    chips, deep = devices // 2, devices // 4
     chip, core = me // 2, me % 2
+    z, y = chip // 2, chip % 2
     sibling = chip * 2 + 1 - core
+    across = (z * 2 + 1 - y) * 2 + core
     slots = send_ref.shape[0] // devices
-    share = up_ref.shape[0] // devices
+    depth = down_out.shape[0]
+    order = list(range(1, deep)) + [0]
+
+    def device_of(hop, row, parity):
+        return (lax.rem(z + hop, deep) * 2 + row) * 2 + parity
+
+    def part(device):
+        columns = pl.ds(pl.multiple_of(device * depth, depth), depth)
+        return leading_product(tokens_ref[:, columns], mix_ref[...])
 
     own = pltpu.make_async_copy(
         send_ref.at[pl.ds(me * slots, slots)], placed_ref.at[pl.ds(me * slots, slots)], own_sem
@@ -185,24 +226,9 @@
     own.start()
     greet_all(me, devices)
 
-    sides = []
-    for offset in list(range(1, chips)) + [0]:
-        target = lax.rem(chip + offset, chips)
-        copy = remote(
-            down_ref.at[target * 2 + 1 - core], side_buf.at[offset],
-            side_send.at[offset], side_recv.at[offset], sibling,
-        )
-        copy.start()
-        sides.append(copy)
-    ups, places = [], []
-    for offset in range(1, devices):
-        peer = lax.rem(me + offset, devices)
-        copy = remote(
-            up_ref.at[pl.ds(peer * share, share)], up_buf.at[offset],
-            up_send.at[offset], up_recv.at[offset], peer,
-        )
-        copy.start()
-        ups.append(copy)
+    up_pair = remote(up_ref.at[:, 1 - core], up_side, up_side_send, up_side_recv, sibling)
+    up_pair.start()
+    places = []
     for offset in range(1, devices):
         peer = lax.rem(me + offset, devices)
         copy = remote(
@@ -212,40 +238,85 @@
         copy.start()
         places.append(copy)
 
-    sent = []
+    sides = []
+    for row in range(2):
+        for hop in order:
+            slot = row * deep + hop
+            part_buf[slot] = part(device_of(hop, 1 - y if row == 0 else y, 1 - core))
+            copy = remote(
+                part_buf.at[slot], side_buf.at[slot], side_send.at[slot], side_recv.at[slot],
+                sibling,
+            )
+            copy.start()
+            sides.append(copy)
+        if row == 0:
+            over = []
+            for hop in order:
+                mine = part(device_of(hop, 1 - y, core))
+                sides[len(over)].wait()
+                y_buf[hop] = (mine + side_buf[hop]).astype(jnp.bfloat16)
+                copy = remote(y_buf.at[hop], y_land.at[hop], y_send.at[hop], y_recv.at[hop], across)
+                copy.start()
+                over.append(copy)
+
+    up_pair.wait()
+    ups = []
     for offset in range(1, chips):
         target = lax.rem(chip + offset, chips)
-        sides[offset - 1].wait()
-        chip_buf[offset] = (down_ref[target * 2 + core] + side_buf[offset]).astype(jnp.bfloat16)
+        up_buf[offset] = up_ref[target, core] + up_side[target]
         copy = remote(
-            chip_buf.at[offset], land_buf.at[offset],
-            chip_send.at[offset], chip_recv.at[offset], target * 2 + core,
+            up_buf.at[offset], up_land.at[offset], up_send.at[offset], up_recv.at[offset],
+            target * 2 + core,
         )
         copy.start()
-        sent.append(copy)
-
-    total = up_ref[pl.ds(pl.multiple_of(me * share, share), share), :]
-    for offset in range(1, devices):
+        ups.append(copy)
+
+    along = []
+    for count, hop in enumerate(order):
+        mine = part(device_of(hop, y, core))
+        sides[deep + count].wait()
+        mine = mine + side_buf[deep + hop]
+        over[count].wait()
+        mine = mine + y_land[hop].astype(jnp.float32)
+        if hop == 0:
+            down_out[...] = mine
+        else:
+            z_buf[hop] = mine.astype(jnp.bfloat16)
+            copy = remote(
+                z_buf.at[hop], z_land.at[hop], z_send.at[hop], z_recv.at[hop],
+                device_of(hop, y, core),
+            )
+            copy.start()
+            along.append(copy)
+
+    total = up_ref[chip, core] + up_side[chip]
+    for offset in range(1, chips):
         ups[offset - 1].wait()
-        total = total + up_buf[offset]
-    up_sum[...] = total * scale
-    up_out[pl.ds(pl.multiple_of(me * share, share), share), :] = total * scale
+        total = total + up_land[offset]
+    up_out[chip, core] = total * scale
     shares = []
-    for offset in range(1, devices):
-        peer = lax.rem(me + offset, devices)
+    for offset in range(1, chips):
+        target = lax.rem(chip + offset, chips)
         copy = remote(
-            up_sum, up_out.at[pl.ds(me * share, share)],
-            share_send.at[offset], share_recv.at[offset], peer,
+            up_out.at[chip, core], up_out.at[chip, core],
+            share_send.at[offset], share_recv.at[offset], target * 2 + core,
         )
         copy.start()
         shares.append(copy)
-
-    sides[chips - 1].wait()
-    down_out[...] = down_ref[me] + side_buf[0]
     for offset in range(1, chips):
-        sent[offset - 1].wait()
-        down_out[...] += land_buf[offset].astype(jnp.float32)
-    down_out[...] *= scale
+        shares[offset - 1].wait_send()
+        place = up_out.at[lax.rem(chip - offset + chips, chips), core]
+        remote(place, place, share_send.at[offset], share_recv.at[offset], sibling).wait_recv()
+    mine_up, other_up = up_out.at[:, core], up_out.at[:, 1 - core]
+    last = remote(mine_up, mine_up, last_send, last_recv, sibling)
+    last.start()
+
+    for copy in along:
+        copy.wait()
+    total = down_out[...]
+    for hop in range(1, deep):
+        total = total + z_land[hop].astype(jnp.float32)
+    down_out[...] = total * scale
 
     own.wait()
     for offset in range(1, devices):
@@ -253,44 +324,52 @@
         places[offset - 1].wait_send()
         place = placed_ref.at[pl.ds(origin * slots, slots)]
         remote(place, place, place_send.at[offset], place_recv.at[offset], sibling).wait_recv()
-        shares[offset - 1].wait_send()
-        place = up_out.at[pl.ds(origin * share, share)]
-        remote(place, place, share_send.at[offset], share_recv.at[offset], sibling).wait_recv()
-
-
-def finish(devices, scale, down_part, up_portion, send_out):
+    last.wait_send()
+    remote(other_up, other_up, last_send, last_recv, sibling).wait_recv()
+
+
+def finish(devices, scale, tokens, mixing_factor, up_portion, send_out):
     dma = pltpu.SemaphoreType.DMA
-    chips = devices // 2
-    depth, width = down_part.shape[0] // devices, down_part.shape[1]
+    chips, deep = devices // 2, devices // 4
+    depth, width = tokens.shape[1] // devices, mixing_factor.shape[1]
     share, features = up_portion.shape[0] // devices, up_portion.shape[1]
     anywhere = pl.BlockSpec(memory_space=pl.ANY)
     local = pl.BlockSpec(memory_space=pltpu.VMEM)
-    return pl.pallas_call(
+    up_shape = (chips, 2, share, features)
+    down, up, placed = pl.pallas_call(
         functools.partial(finish_kernel, devices, scale),
         out_shape=(
             jax.ShapeDtypeStruct((depth, width), jnp.float32),
-            jax.ShapeDtypeStruct(up_portion.shape, jnp.float32),
+            jax.ShapeDtypeStruct(up_shape, jnp.float32),
             jax.ShapeDtypeStruct(send_out.shape, send_out.dtype),
         ),
-        in_specs=[local, local, anywhere],
+        in_specs=[local, local, local, anywhere],
         out_specs=(local, local, anywhere),
         scratch_shapes=[
             pltpu.VMEM((chips, depth, width), jnp.float32),
-            pltpu.VMEM((chips, depth, width), jnp.bfloat16),
-            pltpu.VMEM((chips, depth, width), jnp.bfloat16),
-            pltpu.VMEM((devices, share, features), jnp.float32),
-            pltpu.VMEM((share, features), jnp.float32),
+            pltpu.VMEM((chips, depth, width), jnp.float32),
+            pltpu.VMEM((deep, depth, width), jnp.bfloat16),
+            pltpu.VMEM((deep, depth, width), jnp.bfloat16),
+            pltpu.VMEM((deep, depth, width), jnp.bfloat16),
+            pltpu.VMEM((deep, depth, width), jnp.bfloat16),
+            pltpu.VMEM((chips, share, features), jnp.float32),
+            pltpu.VMEM((chips, share, features), jnp.float32),
+            pltpu.VMEM((chips, share, features), jnp.float32),
             dma,
             dma((devices,)), dma((devices,)),
-            dma((devices,)), dma((devices,)),
-            dma((devices,)), dma((devices,)),
+            dma((chips,)), dma((chips,)),
+            dma((deep,)), dma((deep,)),
+            dma((deep,)), dma((deep,)),
+            dma, dma,
             dma((chips,)), dma((chips,)),
             dma((chips,)), dma((chips,)),
+            dma, dma,
         ],
         compiler_params=pltpu.CompilerParams(
             collective_id=1, has_side_effects=True, vmem_limit_bytes=48 * 1024 * 1024
         ),
-    )(down_part.reshape(devices, depth, width), up_portion, send_out)
+    )(tokens, mixing_factor, up_portion.reshape(up_shape), send_out)
+    return down, up.reshape(up_portion.shape), placed
 
 
 def place_rows(plan, slot_count, per_peer):
@@ -358,13 +437,13 @@
     ).astype(jnp.bfloat16)
     scale = (tokens.shape[0] * devices) ** -0.5
     up_portion = adapter_scale * leading_product(latent_state, row_gradient)
-    down_part = leading_product(tokens, mixing_factor)
     if direct:
         down_grad, up_weight_gradient, placed_out = finish(
-            devices, scale, down_part, up_portion, send_out
+            devices, scale, tokens, mixing_factor, up_portion, send_out
         )
     else:
         placed_out = lax.all_to_all(send_out, "dp", split_axis=0, concat_axis=0, tiled=True)
+        down_part = leading_product(tokens, mixing_factor)
         down_grad = lax.psum_scatter(down_part, "dp", scatter_dimension=0, tiled=True) * scale
         up_weight_gradient = lax.psum(up_portion, "dp") * scale
     return (placed_out, token_gradient, down_grad, up_weight_gradient)

time: 138 us -> 103 us (0.75)
  Pallas kernels: 108 us -> 83.2 us
  local copies, waits for them, and re-layouts: 11.8 us -> 3.26 us
  matrix products: 14.5 us -> 12.7 us
    pallas_call x1, Pallas kernels: 44.1 us -> 29.8 us  [finish(): pl.pallas_call(functools.partial(finish_kernel, devices, scale), out_shap...]
    pallas_call x1, Pallas kernels: 63.7 us -> 53.3 us  [gather_blocks(): pl.pallas_call(functools.partial(gather_kernel, devices), out_shape=(jax....]
    dot_general x1 -> x0, local copies, waits for them, and re-layouts: 5.6 us -> none  [leading_product(): lax.dot_general(left, right, (((0,), (0,)), ((), ())), preferred_element_...]
    unnamed x19 -> x17, local copies, waits for them, and re-layouts: 6.19 us -> 3.26 us
    dot_general x3 -> x2, matrix products: 3.17 us -> 0.49 us  [leading_product(): lax.dot_general(left, right, (((0,), (0,)), ((), ())), preferred_element_...]
where the time goes in v2:
time: 103 us
  Pallas kernels  83.2 us (81%)
  matrix products  12.7 us (12%)
  local copies, waits for them, and re-layouts  3.26 us (3%)
  other arithmetic  2.83 us (3%)
    pallas_call x1, Pallas kernels, gather_blocks(): pl.pallas_call(functools.partial(gather_kernel, devices), out_shape=(jax....  53.3 us
    pallas_call x1, Pallas kernels, finish(): pl.pallas_call(functools.partial(finish_kernel, devices, scale), out_shap...  29.8 us
    dot_general x1, matrix products, shards(): both = jnp.dot(tokens, complete, preferred_element_type=jnp.float32)  6.05 us
    dot_general x2, matrix products, trailing_product(): lax.dot_general(left, right, (((1,), (1,)), ((), ())), preferred_element_...  5.74 us
    unnamed x17, local copies, waits for them, and re-layouts  3.26 us

profile of v2, /device:TPU:0, one launch (start us, length us, event | category | flops | bytes accessed | tf_op | source)
XLA Modules:
  0.0 102.7 jit_solution(15610872803191230176)
XLA Ops:
  0.6 0.0 copy-start
  0.6 0.0 copy-start.1
  0.7 1.0 convert_reduce_fusion
  1.7 0.7 and_select_fusion
  2.3 1.2 %pad_maximum_fusion.block_ref = bf16[512,640]{1,0:T(8,128)(2,1)S(1)} fusion(bf16[512,128]{1,0:T(8,128)(2,1)} %param.11, bf16[512,512]{1,0:T(8,128)(2,1)} %param.10), kind=kLoop, calls=%fused_computation.11 | loop fusion | flops 1310720 | bytes 1310720 | tf_op jit(solution)/shard_map/concatenate | solution.py:413
  3.5 0.0 copy-start.2
  3.5 0.9 copy-done.2
  4.4 53.3 %shard_map.102 = (bf16[8192,640]{1,0:T(8,128)(2,1)}, bf16[256,512]{1,0:T(8,128)(2,1)S(1)}) custom-call(bf16[512,640]{1,0:T(8,128)(2,1)S(1)} %pad_maximum_fusion.block_ref, bf16[256,512]{1,0:T(8,128)(2,1)S(1)} %copy-done.2), custom_call_target="tpu_custom_call" | custom-call | tf_op jit(solution)/shard_map/pallas_call | solution.py:177
  57.8 0.2 convolution_convert_fusion.2
  58.0 0.0 copy-done
  58.0 0.0 slice-start
  58.0 1.0 fusion.3.mix_ref
  59.0 0.0 copy-done.1
  59.0 0.0 slice-start.1
  59.0 0.0 slice-start.2
  59.0 6.0 %convolution_bitcast_fusion = f32[128,640]{1,0:T(8,128)S(1)} fusion(bf16[128,8192]{1,0:T(8,128)(2,1)S(1)} %copy-done.1, bf16[8192,640]{1,0:T(8,128)(2,1)} %get-tuple-element.10), kind=kOutput, calls=%fused_computation.2 | convolution fusion | flops 1342177280 | bytes 12910592 | tf_op jit(solution)/shard_map/dot_general | solution.py:421
  65.1 0.0 slice-done
  65.1 0.0 slice-done.1
  65.1 0.2 slice-done.2
  65.3 0.0 copy-start.3
  65.3 4.7 %convolution_convert_fusion = bf16[128,8192]{1,0:T(8,128)(2,1)} fusion(bf16[8192,640]{1,0:T(8,128)(2,1)S(1)} %bitcast.17, bf16[128,128]{1,0:T(8,128)(2,1)S(1)} %fusion.3.mix_ref, bf16[128,512]{1,0:T(8,128)(2,1)S(1)} %convolution_convert_fusion.2), kind=kOutput, calls=%fused_computation | convolution fusion | flops 1343553536 | bytes 12746752 | tf_op jit(solution)/shard_map/dot_general | solution.py:399
  70.0 0.0 copy-done.3
  70.0 0.3 convolution_multiply_fusion.1
  70.3 0.4 convolution_convert_fusion.1.send_ref
  70.8 29.8 %shard_map.103 = (f32[512,128]{1,0:T(8,128)S(1)}, f32[8,2,8,512]{3,2,1,0:T(8,128)S(1)}, bf16[256,512]{1,0:T(8,128)(2,1)S(1)}) custom-call(bf16[128,8192]{1,0:T(8,128)(2,1)S(1)} %copy-done.1, bf16[128,128]{1,0:T(8,128)(2,1)S(1)} %fusion.3.mix_ref, f32[8,2,8,512]{3,2,1,0:T(8,128)S(1)} %bitcast.14, bf16[256,512]{1,0:T(8,128)(2,1)S(1)} %convolution_convert_fusion.1.send_ref), custom_call_target="tpu_custom_call" | custom-call | tf_op jit(solution)/shard_map/pallas_call | solution.py:339
  100.6 0.7 copy.20
  101.3 0.7 copy.21
  102.0 0.7 copy.22
  (1 shorter events, 0.0 us)
Async XLA Ops:
  0.6 57.4 %copy-start = (bf16[128,512]{1,0:T(8,128)(2,1)S(1)}, bf16[128,512]{1,0:T(8,128)(2,1)}, u32[]{:S(2)}) copy-start(bf16[128,512]{1,0:T(8,128)(2,1)} %param.12) | copy-start | bytes 393220
  0.6 58.4 %copy-start.1 = (bf16[128,8192]{1,0:T(8,128)(2,1)S(1)}, bf16[128,8192]{1,0:T(8,128)(2,1)}, u32[]{:S(2)}) copy-start(bf16[128,8192]{1,0:T(8,128)(2,1)} %tokens_ref.1) | copy-start | bytes 6291460
  3.5 1.0 copy-start.2
  58.0 7.1 %slice-start = ((s8[10485760]{0:T(1024)(128)(4,1)}), s8[4194304]{0:T(1024)(128)(4,1)S(1)}, s32[]{:S(2)}) async-start(s8[10485760]{0:T(1024)(128)(4,1)} %bitcast.16), calls=%async_computation | async-start | bytes 8388608
  59.0 6.1 %slice-start.1 = ((s8[10485760]{0:T(1024)(128)(4,1)}), s8[4194304]{0:T(1024)(128)(4,1)S(1)}, s32[]{:S(2)}) async-start(s8[10485760]{0:T(1024)(128)(4,1)} %bitcast.16), calls=%async_computation.1 | async-start | bytes 8388608
  59.0 6.3 %slice-start.2 = ((s8[10485760]{0:T(1024)(128)(4,1)}), s8[2097152]{0:T(1024)(128)(4,1)S(1)}, s32[]{:S(2)}) async-start(s8[10485760]{0:T(1024)(128)(4,1)} %bitcast.16), calls=%async_computation.2 | async-start | bytes 4194304
  65.3 4.8 %copy-start.3 = (s32[128]{0:T(128)S(1)}, s32[128]{0:T(128)}, u32[]{:S(2)}) copy-start(s32[128]{0:T(128)} %param.8) | copy-start | bytes 1540

commit v3 on v2

--- a/solution.py
+++ b/solution.py
@@ -228,6 +228,18 @@
 
     up_pair = remote(up_ref.at[:, 1 - core], up_side, up_side_send, up_side_recv, sibling)
     up_pair.start()
+    up_pair.wait()
+    ups = []
+    for offset in range(1, chips):
+        target = lax.rem(chip + offset, chips)
+        up_buf[offset] = up_ref[target, core] + up_side[target]
+        copy = remote(
+            up_buf.at[offset], up_land.at[offset], up_send.at[offset], up_recv.at[offset],
+            target * 2 + core,
+        )
+        copy.start()
+        ups.append(copy)
+
     places = []
     for offset in range(1, devices):
         peer = lax.rem(me + offset, devices)
@@ -258,18 +270,6 @@
                 copy = remote(y_buf.at[hop], y_land.at[hop], y_send.at[hop], y_recv.at[hop], across)
                 copy.start()
                 over.append(copy)
-
-    up_pair.wait()
-    ups = []
-    for offset in range(1, chips):
-        target = lax.rem(chip + offset, chips)
-        up_buf[offset] = up_ref[target, core] + up_side[target]
-        copy = remote(
-            up_buf.at[offset], up_land.at[offset], up_send.at[offset], up_recv.at[offset],
-            target * 2 + core,
-        )
-        copy.start()
-        ups.append(copy)
 
     along = []
     for count, hop in enumerate(order):

time: 103 us -> 104 us (level)
  Pallas kernels: 83.2 us -> 84.6 us
    pallas_call x1, Pallas kernels: 29.8 us -> 31.2 us  [finish(): pl.pallas_call(functools.partial(finish_kernel, devices, scale), out_shap...]
where the time goes in v3:
time: 104 us
  Pallas kernels  84.6 us (81%)
  matrix products  12.7 us (12%)
  local copies, waits for them, and re-layouts  3.26 us (3%)
  other arithmetic  2.83 us (3%)
    pallas_call x1, Pallas kernels, gather_blocks(): pl.pallas_call(functools.partial(gather_kernel, devices), out_shape=(jax....  53.3 us
    pallas_call x1, Pallas kernels, finish(): pl.pallas_call(functools.partial(finish_kernel, devices, scale), out_shap...  31.2 us
    dot_general x1, matrix products, shards(): both = jnp.dot(tokens, complete, preferred_element_type=jnp.float32)  6.05 us
    dot_general x2, matrix products, trailing_product(): lax.dot_general(left, right, (((1,), (1,)), ((), ())), preferred_element_...  5.74 us
    unnamed x17, local copies, waits for them, and re-layouts  3.26 us

profile of v3, /device:TPU:0, one launch (start us, length us, event | category | flops | bytes accessed | tf_op | source)
XLA Modules:
  0.0 104.1 jit_solution(13302642387388851542)
XLA Ops:
  0.6 0.0 copy-start
  0.6 0.0 copy-start.1
  0.7 1.0 convert_reduce_fusion
  1.7 0.7 and_select_fusion
  2.3 1.2 %pad_maximum_fusion.block_ref = bf16[512,640]{1,0:T(8,128)(2,1)S(1)} fusion(bf16[512,128]{1,0:T(8,128)(2,1)} %param.11, bf16[512,512]{1,0:T(8,128)(2,1)} %param.10), kind=kLoop, calls=%fused_computation.11 | loop fusion | flops 1310720 | bytes 1310720 | tf_op jit(solution)/shard_map/concatenate | solution.py:413
  3.5 0.0 copy-start.2
  3.5 0.9 copy-done.2
  4.4 53.3 %shard_map.102 = (bf16[8192,640]{1,0:T(8,128)(2,1)}, bf16[256,512]{1,0:T(8,128)(2,1)S(1)}) custom-call(bf16[512,640]{1,0:T(8,128)(2,1)S(1)} %pad_maximum_fusion.block_ref, bf16[256,512]{1,0:T(8,128)(2,1)S(1)} %copy-done.2), custom_call_target="tpu_custom_call" | custom-call | tf_op jit(solution)/shard_map/pallas_call | solution.py:177
  57.8 0.2 convolution_convert_fusion.2
  58.0 0.0 copy-done
  58.0 0.0 slice-start
  58.0 1.0 fusion.3.mix_ref
  59.0 0.0 copy-done.1
  59.0 0.0 slice-start.1
  59.0 0.0 slice-start.2
  59.0 6.0 %convolution_bitcast_fusion = f32[128,640]{1,0:T(8,128)S(1)} fusion(bf16[128,8192]{1,0:T(8,128)(2,1)S(1)} %copy-done.1, bf16[8192,640]{1,0:T(8,128)(2,1)} %get-tuple-element.10), kind=kOutput, calls=%fused_computation.2 | convolution fusion | flops 1342177280 | bytes 12910592 | tf_op jit(solution)/shard_map/dot_general | solution.py:421
  65.1 0.0 slice-done
  65.1 0.0 slice-done.1
  65.1 0.2 slice-done.2
  65.3 0.0 copy-start.3
  65.3 4.7 %convolution_convert_fusion = bf16[128,8192]{1,0:T(8,128)(2,1)} fusion(bf16[8192,640]{1,0:T(8,128)(2,1)S(1)} %bitcast.17, bf16[128,128]{1,0:T(8,128)(2,1)S(1)} %fusion.3.mix_ref, bf16[128,512]{1,0:T(8,128)(2,1)S(1)} %convolution_convert_fusion.2), kind=kOutput, calls=%fused_computation | convolution fusion | flops 1343553536 | bytes 12746752 | tf_op jit(solution)/shard_map/dot_general | solution.py:399
  70.0 0.0 copy-done.3
  70.0 0.3 convolution_multiply_fusion.1
  70.3 0.4 convolution_convert_fusion.1.send_ref
  70.8 31.2 %shard_map.103 = (f32[512,128]{1,0:T(8,128)S(1)}, f32[8,2,8,512]{3,2,1,0:T(8,128)S(1)}, bf16[256,512]{1,0:T(8,128)(2,1)S(1)}) custom-call(bf16[128,8192]{1,0:T(8,128)(2,1)S(1)} %copy-done.1, bf16[128,128]{1,0:T(8,128)(2,1)S(1)} %fusion.3.mix_ref, f32[8,2,8,512]{3,2,1,0:T(8,128)S(1)} %bitcast.14, bf16[256,512]{1,0:T(8,128)(2,1)S(1)} %convolution_convert_fusion.1.send_ref), custom_call_target="tpu_custom_call" | custom-call | tf_op jit(solution)/shard_map/pallas_call | solution.py:339
  102.0 0.7 copy.20
  102.7 0.7 copy.21
  103.4 0.7 copy.22
  (1 shorter events, 0.0 us)
Async XLA Ops:
  0.6 57.4 %copy-start = (bf16[128,512]{1,0:T(8,128)(2,1)S(1)}, bf16[128,512]{1,0:T(8,128)(2,1)}, u32[]{:S(2)}) copy-start(bf16[128,512]{1,0:T(8,128)(2,1)} %param.12) | copy-start | bytes 393220
  0.6 58.4 %copy-start.1 = (bf16[128,8192]{1,0:T(8,128)(2,1)S(1)}, bf16[128,8192]{1,0:T(8,128)(2,1)}, u32[]{:S(2)}) copy-start(bf16[128,8192]{1,0:T(8,128)(2,1)} %tokens_ref.1) | copy-start | bytes 6291460
  3.5 1.0 copy-start.2
  58.0 7.1 %slice-start = ((s8[10485760]{0:T(1024)(128)(4,1)}), s8[4194304]{0:T(1024)(128)(4,1)S(1)}, s32[]{:S(2)}) async-start(s8[10485760]{0:T(1024)(128)(4,1)} %bitcast.16), calls=%async_computation | async-start | bytes 8388608
  59.0 6.1 %slice-start.1 = ((s8[10485760]{0:T(1024)(128)(4,1)}), s8[4194304]{0:T(1024)(128)(4,1)S(1)}, s32[]{:S(2)}) async-start(s8[10485760]{0:T(1024)(128)(4,1)} %bitcast.16), calls=%async_computation.1 | async-start | bytes 8388608
  59.0 6.3 %slice-start.2 = ((s8[10485760]{0:T(1024)(128)(4,1)}), s8[2097152]{0:T(1024)(128)(4,1)S(1)}, s32[]{:S(2)}) async-start(s8[10485760]{0:T(1024)(128)(4,1)} %bitcast.16), calls=%async_computation.2 | async-start | bytes 4194304
  65.3 4.8 %copy-start.3 = (s32[128]{0:T(128)S(1)}, s32[128]{0:T(128)}, u32[]{:S(2)}) copy-start(s32[128]{0:T(128)} %param.8) | copy-start | bytes 1540
